TPU v7x, 32 devices: a whole 2x2x4 slice. The times are simulated.
32 devices in a mesh: groups: 2 (over y), cand: 4 (over x, core), hist: 4 (over z).
Axes of the slice: x: 2, y: 2, z: 4, core: 2. Of those that a mesh axis runs over, the one named last changes fastest.
Arguments:
- cand_feats: bfloat16 [2048, 256], P(('groups', 'cand')), parts along dimension 0, may hold values from -6 to 6
- cat_table: bfloat16 [4, 256], P('groups'), parts along dimension 0, may hold values from -5 to 5
- cand_cat: int32 [2048], P(('groups', 'cand')), parts along dimension 0, may hold values from 0 to 1
- cand_blocks: int32 [2048, 16], P(('groups', 'cand')), parts along dimension 0, may hold values from 0 to 127, as said below
- cand_count: int32 [2048], P(('groups', 'cand')), parts along dimension 0, may hold values from 1 to 16
- keys: bfloat16 [32768, 256], P(('groups', 'cand', 'hist')), parts along dimension 0, may hold values from -6 to 6
- values: bfloat16 [32768, 256], P(('groups', 'cand', 'hist')), parts along dimension 0, may hold values from -6 to 6
- w_query: bfloat16 [256, 256], replicated, may hold values from -0.375 to 0.375
- norm_gain: float32 [256], replicated, may hold values from 0.25 to 1.75
- w_up: bfloat16 [256, 1024], replicated, may hold values from -0.375 to 0.375
- w_down: bfloat16 [1024, 256], replicated, may hold values from -0.1875 to 0.1875
Outputs:
- ranked: bfloat16 [2048, 256], P(('groups', 'cand')), parts along dimension 0
There are 2 independent parts, one for each index of `groups`. A program takes and returns all parts, laid end to end along the dimension named above; an argument that names none is the same for every part. Nothing has to cross between parts.
Inputs may be any that keep to these rules, and one draw needn't show every extreme that they name: `cand_blocks`: block b has category b % 2; every block a candidate lists has the candidate's category, and the 16 ids in one row are distinct. Some candidate uses all 16 slots and some only one.
All inputs are finite; a program needn't handle non-finite values.
Results may differ from a plain program's by a relative error of at most 0.0055.
Values may be sent and summed in bfloat16 or wider, within the bound.
A program may use at most 64 MiB of HBM per device.

v0:
```python
import math

import jax
import jax.numpy as jnp
from jax import lax
from jax.sharding import PartitionSpec as P

HEADS = 4
BLOCK = 128


def passed_along(block, axis, distance):
    devices = range(lax.axis_size(axis))
    route = [((i - distance) % len(devices), i) for i in devices]
    return lax.ppermute(block, axis, route)


def finish(attended, feat_rows, norm_gain, w_up, w_down):
    mean_square = jnp.mean(attended * attended, axis=-1, keepdims=True)
    normed = (attended * lax.rsqrt(mean_square + 1e-06) * norm_gain).astype(jnp.bfloat16)
    hidden = jax.nn.silu(jnp.dot(normed, w_up, preferred_element_type=jnp.float32)).astype(
        jnp.bfloat16
    )
    result = feat_rows.astype(jnp.float32) + jnp.dot(
        hidden, w_down, preferred_element_type=jnp.float32
    )
    return result.astype(jnp.bfloat16)


def partial_attend(
    query_part, lists_part, key_part, value_part, block_ids, head_count, block_rows, score_scale
):
    row_count = query_part.shape[0]
    model_width = query_part.shape[1]
    head_width = model_width // head_count
    key_count = key_part.shape[0]
    blocks_here = block_ids.shape[0]
    member = jnp.any(lists_part[:, :, None] == block_ids[None, None, :], axis=1)
    block_mask = jnp.broadcast_to(member[:, :, None], (row_count, blocks_here, block_rows))
    block_mask = block_mask.reshape(row_count, key_count).astype(jnp.float32)
    query_heads = query_part.reshape(row_count, head_count, head_width)
    key_heads = key_part.reshape(key_count, head_count, head_width)
    value_heads = value_part.reshape(key_count, head_count, head_width)
    scores = (
        jnp.einsum("chd,jhd->hcj", query_heads, key_heads, preferred_element_type=jnp.float32)
        * score_scale
    )
    weights_bf = (jax.nn.silu(scores) * block_mask[None]).astype(jnp.bfloat16)
    return jnp.einsum("hcj,jhd->chd", weights_bf, value_heads, preferred_element_type=jnp.float32)


def shards(
    cand_feats,
    cat_table,
    cand_cat,
    cand_blocks,
    cand_count,
    keys,
    values,
    w_query,
    norm_gain,
    w_up,
    w_down,
):
    cand_rows = cand_feats.shape[0]
    cat_count = cat_table.shape[0]
    head_count = HEADS
    model_width = cand_feats.shape[1]
    head_width = model_width // head_count
    piece_rows = keys.shape[0]
    block_rows = BLOCK
    blocks_here = piece_rows // block_rows
    cycle_size = lax.axis_size("cand")
    hist_size = lax.axis_size("hist")
    cand_index = lax.axis_index("cand")
    hist_index = lax.axis_index("hist")
    score_scale = 1.0 / math.sqrt(head_width)
    onehot = (cand_cat[:, None] == jnp.arange(cat_count, dtype=jnp.int32)[None, :]).astype(
        jnp.bfloat16
    )
    embedded = jnp.dot(onehot, cat_table, preferred_element_type=jnp.float32)
    query_input = (cand_feats.astype(jnp.float32) + embedded).astype(jnp.bfloat16)
    query_flat = jnp.dot(query_input, w_query, preferred_element_type=jnp.float32).astype(
        jnp.bfloat16
    )
    slot_live = jnp.arange(cand_blocks.shape[1], dtype=jnp.int32)[None, :] < cand_count[:, None]
    live_lists = jnp.where(slot_live, cand_blocks, -1)

    def owned_ids(owner):
        return (owner * hist_size + hist_index) * blocks_here + jnp.arange(
            blocks_here, dtype=jnp.int32
        )

    def attend(running, kv_piece, owner):
        return running + partial_attend(
            query_flat,
            live_lists,
            kv_piece[0],
            kv_piece[1],
            owned_ids(owner),
            head_count,
            block_rows,
            score_scale,
        )

    kv_local = jnp.stack([keys, values])
    running = jnp.zeros((cand_rows, head_count, head_width), jnp.float32)
    running = attend(running, kv_local, cand_index)

    def turn_one(turn_index, state_tuple):
        kv_piece, partial_run = state_tuple
        kv_piece = passed_along(kv_piece, "cand", 1)
        return (kv_piece, attend(partial_run, kv_piece, (cand_index - turn_index) % cycle_size))

    kv_last, running = lax.fori_loop(1, cycle_size, turn_one, (kv_local, running))
    partial_sum = running.reshape(cand_rows, model_width)
    attended = lax.psum(partial_sum, "hist")
    return finish(attended, cand_feats, norm_gain, w_up, w_down)


def solution(mesh):
    in_specs = (
        P(("groups", "cand"), None),
        P("groups", None),
        P(("groups", "cand")),
        P(("groups", "cand"), None),
        P(("groups", "cand")),
        P(("groups", "cand", "hist"), None),
        P(("groups", "cand", "hist"), None),
        P(),
        P(),
        P(),
        P(),
    )
    out_specs = P(("groups", "cand"), None)
    return jax.shard_map(shards, mesh=mesh, in_specs=in_specs, out_specs=out_specs, check_vma=False)
```

profile of v0, /device:TPU:0, one launch (start us, length us, event | category | flops | bytes accessed | tf_op | source)
XLA Modules:
  0.0 120.5 jit_solution(3753762689150936511)
XLA Ops:
  6.5 0.8 fusion.17
  7.3 0.1 compare_reduce_fusion.1
  7.4 0.1 copy.28
  7.6 0.3 broadcast_in_dim.48
  7.9 0.0 copy-start.1
  7.9 0.2 copy.35
  8.1 0.8 copy-done.1
  8.9 0.2 copy.25
  9.2 0.2 copy.26
  9.4 1.1 pad_maximum_fusion
  10.5 0.4 convolution_convert_fusion
  10.9 2.0 %fusion.6 = f32[256,4,64]{0,2,1:T(8,128)S(1)} fusion(bf16[1024,4,64]{0,2,1:T(8,128)(2,1)S(1)} %bitcast.59, bf16[256,4,64]{0,2,1:T(8,128)(2,1)S(1)} %bitcast.62, bf16[1024,4,64]{0,2,1:T(8,128)(2,1)S(1)} %bitcast.57, f32[256,1024]{1,0:T(8,128)S(1)} %bitcast.60), kind=kOutput, calls=%fused_computation.13 | convolution fusion | flops 275775488 | bytes 2490368 | tf_op jit(solution)/shard_map/hcj,jhd->chd/dot_general | solution.py:49
  12.9 59.1 %while.17 = (s32[]{:T(128)}, bf16[2,1024,256]{1,2,0:T(8,128)(2,1)}, f32[256,4,64]{0,2,1:T(8,128)S(1)}, bf16[256,256]{0,1:T(8,128)(2,1)S(1)}, s32[256,16]{0,1:T(8...) while((s32[]{:T(128)}, bf16[2,1024,256]{1,2,0:T(8,128)(2,1)}, ...), condition=%wide.region_3.4_spmd, body=%wide.region_1.3_spmd.sunk | while | flops 275906592 | bytes 15389110 | solution.py:115
  12.9 0.5 collective-permute-start
  13.4 0.1 compare_reduce_fusion.3
  13.5 0.1 copy.38
  13.7 0.3 broadcast_in_dim.51
  14.0 0.2 copy.39
  14.2 13.8 %collective-permute-done = bf16[2,1024,256]{1,2,0:T(8,128)(2,1)S(1)} collective-permute-done((bf16[2,1024,256]{1,2,0:T(8,128)(2,1)}, bf16[2,1024,256]{1,2,0:T(8,128)(2,1)S(1)}, u32[]{:S(2)}, u32[]{:S(2)}) %collective-permute-start) | collective-permute-done | bytes 1048608 | tf_op jit(solution)/shard_map/while/body/eval_jaxpr/ppermute | solution.py:15
  28.1 0.9 fusion.40
  28.9 3.1 %fusion.41 = f32[256,4,64]{0,2,1:T(8,128)S(1)} fusion(f32[256,4,64]{0,2,1:T(8,128)S(1)} %get-tuple-element.260, bf16[1024,4,64]{0,2,1:T(8,128)(2,1)} %bitcast.54, bf16[256,4,64]{0,2,1:T(8,128)(2,1)} %bitcast.63, bf16[1024,4,64]{0,2,1:T(8,128)(2,1)S(1)} %bitcast.53, f32[256,1024]{1,0:T(8,128)S(1)} %bitcast.52), kind=kOutput, calls=%fused_computation.3.clone.1 | convolution fusion | flops 275841024 | bytes 2752512 | tf_op jit(solution)/shard_map/while/body/eval_jaxpr/hcj,jhd->chd/dot_general | solution.py:49
  32.1 1.0 copy.47
  33.0 0.0 copy-done.7
  33.1 0.0 collective-permute-start
  33.1 0.1 compare_reduce_fusion.3
  33.2 0.1 copy.38
  33.4 0.3 broadcast_in_dim.51
  33.7 0.2 copy.39
  33.9 13.6 %collective-permute-done = bf16[2,1024,256]{1,2,0:T(8,128)(2,1)S(1)} collective-permute-done((bf16[2,1024,256]{1,2,0:T(8,128)(2,1)}, bf16[2,1024,256]{1,2,0:T(8,128)(2,1)S(1)}, u32[]{:S(2)}, u32[]{:S(2)}) %collective-permute-start) | collective-permute-done | bytes 1048608 | tf_op jit(solution)/shard_map/while/body/eval_jaxpr/ppermute | solution.py:15
  47.5 0.9 fusion.40
  48.4 3.1 %fusion.41 = f32[256,4,64]{0,2,1:T(8,128)S(1)} fusion(f32[256,4,64]{0,2,1:T(8,128)S(1)} %get-tuple-element.260, bf16[1024,4,64]{0,2,1:T(8,128)(2,1)} %bitcast.54, bf16[256,4,64]{0,2,1:T(8,128)(2,1)} %bitcast.63, bf16[1024,4,64]{0,2,1:T(8,128)(2,1)S(1)} %bitcast.53, f32[256,1024]{1,0:T(8,128)S(1)} %bitcast.52), kind=kOutput, calls=%fused_computation.3.clone.1 | convolution fusion | flops 275841024 | bytes 2752512 | tf_op jit(solution)/shard_map/while/body/eval_jaxpr/hcj,jhd->chd/dot_general | solution.py:49
  51.5 1.0 copy.47
  52.5 0.0 copy-done.7
  52.5 0.0 collective-permute-start
  52.6 0.1 compare_reduce_fusion.3
  52.7 0.1 copy.38
  52.8 0.3 broadcast_in_dim.51
  53.1 0.2 copy.39
  53.4 13.6 %collective-permute-done = bf16[2,1024,256]{1,2,0:T(8,128)(2,1)S(1)} collective-permute-done((bf16[2,1024,256]{1,2,0:T(8,128)(2,1)}, bf16[2,1024,256]{1,2,0:T(8,128)(2,1)S(1)}, u32[]{:S(2)}, u32[]{:S(2)}) %collective-permute-start) | collective-permute-done | bytes 1048608 | tf_op jit(solution)/shard_map/while/body/eval_jaxpr/ppermute | solution.py:15
  67.0 0.9 fusion.40
  67.8 3.1 %fusion.41 = f32[256,4,64]{0,2,1:T(8,128)S(1)} fusion(f32[256,4,64]{0,2,1:T(8,128)S(1)} %get-tuple-element.260, bf16[1024,4,64]{0,2,1:T(8,128)(2,1)} %bitcast.54, bf16[256,4,64]{0,2,1:T(8,128)(2,1)} %bitcast.63, bf16[1024,4,64]{0,2,1:T(8,128)(2,1)S(1)} %bitcast.53, f32[256,1024]{1,0:T(8,128)S(1)} %bitcast.52), kind=kOutput, calls=%fused_computation.3.clone.1 | convolution fusion | flops 275841024 | bytes 2752512 | tf_op jit(solution)/shard_map/while/body/eval_jaxpr/hcj,jhd->chd/dot_general | solution.py:49
  71.0 1.0 copy.47
  71.9 0.0 copy-done.7
  72.0 0.7 copy-done.3
  72.7 0.0 all-reduce.2.cloned.1.call-update
  72.7 37.5 %all-reduce.2.cloned.1.call-done = f32[256,256]{0,1:T(8,128)} async-done(((f32[256,256]{0,1:T(8,128)}), f32[256,256]{0,1:T(8,128)}) %all-reduce.2.cloned.1.call-update) | async-done | bytes 262160 | tf_op jit(solution)/shard_map/psum | solution.py:117
  110.2 1.0 multiply_reduce_fusion
  111.2 2.5 %fusion.7 = bf16[256,256]{1,0:T(8,128)(2,1)} fusion(bf16[1024,256]{1,0:T(8,128)(2,1)S(1)} %copy-done, bf16[256,256]{1,0:T(8,128)(2,1)S(1)} %copy-done.5, bf16[256,1024]{1,0:T(8,128)(2,1)} %param.22, f32[256,256]{0,1:T(8,128)} %all-reduce.2.cloned.1.call-done, f32[256]{0:T(256)} %param.21, f32[256]{0:T(256)S(1)} %add_rsqrt_fusion), kind=kOutput, calls=%fused_computation.14 | convolution fusion | flops 270139392 | bytes 1574912 | tf_op jit(solution)/shard_map/dot_general | solution.py:24
  (32 shorter events, 0.1 us)
Async XLA Ops:
  6.5 104.7 %copy-start = (bf16[1024,256]{1,0:T(8,128)(2,1)S(1)}, bf16[1024,256]{1,0:T(8,128)(2,1)}, u32[]{:S(2)}) copy-start(bf16[1024,256]{1,0:T(8,128)(2,1)} %param.23) | copy-start | bytes 1572868
  6.5 103.7 %all-reduce.2.cloned.1.call-start = ((), (), s32[]{:S(2)}) async-start(), calls=%async_computation | async-start | bytes 524288 | tf_op jit(solution)/shard_map/psum | solution.py:117
  7.9 1.0 copy-start.1
  7.9 1.2 %copy-start.2 = (bf16[1024,256]{1,0:T(8,128)(2,1)S(1)}, bf16[1024,256]{1,0:T(8,128)(2,1)}, u32[]{:S(2)}) copy-start(bf16[1024,256]{1,0:T(8,128)(2,1)} %param.19) | copy-start | bytes 1572868
  9.4 1.1 copy-start.4
  9.4 1.1 copy-start.5
  9.4 1.1 copy-start.8
  9.4 1.1 copy-start.9
  12.9 1.3 %copy-start.6 = (bf16[256,256]{0,1:T(8,128)(2,1)}, bf16[256,256]{0,1:T(8,128)(2,1)S(1)}, u32[]{:S(2)}) copy-start(bf16[256,256]{0,1:T(8,128)(2,1)S(1)} %get-tuple-element.273) | copy-start | bytes 393220 | tf_op jit(solution)/shard_map/while
  12.9 15.1 %collective-permute-start = (bf16[2,1024,256]{1,2,0:T(8,128)(2,1)}, bf16[2,1024,256]{1,2,0:T(8,128)(2,1)S(1)}, u32[]{:S(2)}, u32[]{:S(2)}) collective-permute-start(bf16[2,1024,256]{1,2,0:T(8,128)(2,1)} %get-tuple-element.259), channel_id=1, source_target_pairs={{12,0},{0,4},{4,8},{8,12},{13,1},{1,5},{5,9},{9,13},{14,2},{2,6},{... | collective-permute-start | bytes 3145736 | tf_op jit(solution)/shard_map/while/body/eval_jaxpr/ppermute | solution.py:15
  32.1 1.0 copy-start.7
  33.1 0.8 copy-start.6
  33.1 14.4 %collective-permute-start = (bf16[2,1024,256]{1,2,0:T(8,128)(2,1)}, bf16[2,1024,256]{1,2,0:T(8,128)(2,1)S(1)}, u32[]{:S(2)}, u32[]{:S(2)}) collective-permute-start(bf16[2,1024,256]{1,2,0:T(8,128)(2,1)} %get-tuple-element.259), channel_id=1, source_target_pairs={{12,0},{0,4},{4,8},{8,12},{13,1},{1,5},{5,9},{9,13},{14,2},{2,6},{... | collective-permute-start | bytes 3145736 | tf_op jit(solution)/shard_map/while/body/eval_jaxpr/ppermute | solution.py:15
  51.5 1.0 copy-start.7
  52.5 0.8 copy-start.6
  52.5 14.4 %collective-permute-start = (bf16[2,1024,256]{1,2,0:T(8,128)(2,1)}, bf16[2,1024,256]{1,2,0:T(8,128)(2,1)S(1)}, u32[]{:S(2)}, u32[]{:S(2)}) collective-permute-start(bf16[2,1024,256]{1,2,0:T(8,128)(2,1)} %get-tuple-element.259), channel_id=1, source_target_pairs={{12,0},{0,4},{4,8},{8,12},{13,1},{1,5},{5,9},{9,13},{14,2},{2,6},{... | collective-permute-start | bytes 3145736 | tf_op jit(solution)/shard_map/while/body/eval_jaxpr/ppermute | solution.py:15
  71.0 1.0 copy-start.7
  72.0 0.7 copy-start.3
Sparse Core Ops, SparseCore 0:
  72.8 37.3 all-reduce.1
where the time goes:
time: 121 us
  waiting for transfers between devices  78.5 us (65%)
  matrix products  14.3 us (12%)
  between operations  13.5 us (11%)
  local copies, waits for them, and re-layouts  10.2 us (8%)
  other arithmetic  3.25 us (3%)
    ppermute x3, waiting for transfers between devices, passed_along(): return lax.ppermute(block, axis, route)  41 us
    psum x1, waiting for transfers between devices, shards(): attended = lax.psum(partial_sum, 'hist')  37.5 us
    dot_general x4, matrix products, partial_attend(): jnp.einsum('hcj,jhd->chd', weights_bf, value_heads, preferred_element_typ...  11.4 us
    while x18, local copies, waits for them, and re-layouts  3.59 us
    slice x3, local copies, waits for them, and re-layouts, attend(): kv_piece[0]  2.6 us
    dot_general x1, matrix products, finish(): jnp.dot(hidden, w_down, preferred_element_type=jnp.float32)  2.46 us
  transfers between devices with their start and end apart: 4, of which 4 were waited for; matrix products, arithmetic and copies ran while one was open for 2% of the time, Pallas kernels for 0%

commit v1 on v0

v1 whole, which is shorter than its diff:
```python
import functools
import math

import jax
import jax.numpy as jnp
from jax import lax
from jax.experimental import pallas as pl
from jax.experimental.pallas import tpu as pltpu
from jax.sharding import PartitionSpec as P

HEADS = 4
BLOCK = 128
CORES = 2
LANES = 128
FAR = -(2.0**30)
F32 = jnp.float32
BF16 = jnp.bfloat16
MESH = pl.DeviceIdType.MESH


def dot(a, b, contract):
    return lax.dot_general(a, b, ((contract[:1], contract[1:]), ((), ())), preferred_element_type=F32)


def kernel(
    chips, depth,
    feats, table, cat, lists, count, keys, values, w_query, gain, w_up, w_down,
    out,
    feats_v, wq_v, up_v, down_v, kv, key_mix, value_mix, query_v, query_in, mask_v, mask_in,
    total, part_out, part_in, slice_out, slice_in,
    load_sem, pair_send, pair_recv, query_send, query_recv, mask_send, mask_recv,
    part_send, part_recv, slice_send, slice_recv, out_send, out_recv,
):
    rows, width = feats.shape
    head_width = width // HEADS
    tile_heads = LANES // head_width
    tiles = width // LANES
    blocks = keys.shape[0] // BLOCK
    pairs = blocks // 2
    chunk = rows // depth
    cand = lax.axis_index("cand")
    hist = lax.axis_index("hist")
    chip = cand // CORES
    core = cand % CORES
    partner = {"cand": cand + 1 - 2 * core}

    def x_peer(step):
        return {"cand": ((chip + step + chips) % chips) * CORES + core}

    def z_peer(step):
        return {"hist": (hist + step) % depth}

    barrier = pltpu.get_barrier_semaphore()
    peers = [partner] + [x_peer(j) for j in range(1, chips)] + [z_peer(k) for k in range(1, depth)]
    for peer in peers:
        pl.semaphore_signal(barrier, inc=1, device_id=peer, device_id_type=MESH)

    pieces = [(feats, feats_v), (w_query, wq_v), (keys, kv.at[0]), (values, kv.at[1]), (w_up, up_v), (w_down, down_v)]
    loads = [pltpu.make_async_copy(a, b, load_sem.at[i]) for i, (a, b) in enumerate(pieces)]
    for load in loads:
        load.start()

    def remote(src, dst, send, recv, peer):
        return pltpu.make_async_remote_copy(
            src_ref=src, dst_ref=dst, send_sem=send, recv_sem=recv, device_id=peer, device_id_type=MESH
        )

    category = cat[...]
    slots = lax.broadcasted_iota(jnp.int32, lists.shape, 0)
    live = jnp.where(slots < count[...], lists[...], -1)
    row_id = lax.broadcasted_iota(jnp.int32, (16, rows), 0)
    for j in range(chips):
        owner_chip = (chip + j) % chips
        mask = jnp.where(row_id == CORES * pairs, category.astype(F32), 0.0)
        for r in range(CORES * pairs):
            owner = owner_chip * CORES + r // pairs
            wanted = (owner * depth + hist) * blocks + 2 * (r % pairs) + category
            missing = jnp.min(jnp.where(live == wanted, 0.0, 1.0), axis=0, keepdims=True)
            mask = jnp.where(row_id == r, missing, mask)
        mask_v[j] = mask.astype(BF16)

    spread_row = lax.broadcasted_iota(jnp.int32, (16, 2 * LANES), 0)
    spread_lane = lax.broadcasted_iota(jnp.int32, (16, 2 * LANES), 1)
    spread = jnp.where(
        spread_lane < LANES,
        jnp.where((spread_lane % head_width == spread_row) & (spread_row < CORES * pairs), 1.0, 0.0),
        jnp.where(spread_row == CORES * pairs, 1.0, 0.0),
    ).astype(BF16)

    def expand(mask):
        both = dot(mask, spread, (0, 0))
        return both[:, :LANES].astype(BF16), both[:, LANES:]

    own_mask, own_second = expand(mask_v[0])

    loads[0].wait()
    loads[1].wait()
    table_f = table[...].astype(F32)
    inputs = []
    for t in range(tiles):
        cut = slice(t * LANES, (t + 1) * LANES)
        embedded = jnp.where(own_second > 0.5, table_f[1:2, cut], table_f[0:1, cut])
        inputs.append((feats_v[:, cut].astype(F32) + embedded).astype(BF16))
    scale = 0.5 / math.sqrt(head_width)
    query_v[...] = (dot(jnp.concatenate(inputs, axis=1), wq_v[...], (1, 0)) * scale).astype(BF16)

    pl.semaphore_wait(barrier, len(peers))
    query_copies, mask_copies = [], []
    for j in range(1, chips):
        query_copies.append(remote(query_v, query_in.at[j - 1], query_send.at[j - 1], query_recv.at[j - 1], x_peer(j)))
        mask_copies.append(remote(mask_v.at[j], mask_in.at[j - 1], mask_send.at[j - 1], mask_recv.at[j - 1], x_peer(j)))
        mask_copies[-1].start()
        query_copies[-1].start()
    pair_copies = [
        remote(keys, kv.at[2], pair_send.at[0], pair_recv.at[0], partner),
        remote(values, kv.at[3], pair_send.at[1], pair_recv.at[1], partner),
    ]
    for copy in pair_copies:
        copy.start()

    lane = lax.broadcasted_iota(jnp.int32, (1, LANES), 1)
    head_lane = [jnp.where(lane // head_width == a, 1.0, 0.0).astype(BF16) for a in range(tile_heads)]
    other_lane = [jnp.where(lane // head_width == a, 0.0, 1.0).astype(BF16) for a in range(tile_heads)]

    def mix_keys(side):
        owner = core if side == 0 else 1 - core
        for p in range(pairs):
            dst = slice(p * BLOCK, (p + 1) * BLOCK)
            even = slice(2 * p * BLOCK, (2 * p + 1) * BLOCK)
            odd = slice((2 * p + 1) * BLOCK, (2 * p + 2) * BLOCK)
            for t in range(tiles):
                cut = slice(t * LANES, (t + 1) * LANES)
                first, second = kv[2 * side, even, cut], kv[2 * side, odd, cut]
                for a in range(tile_heads):
                    spot = ((a + 1) % tile_heads) * head_width + owner * pairs + p
                    away = jnp.where(lane == spot, FAR, 0.0).astype(BF16)
                    key_mix[side, t * tile_heads + a, dst, :LANES] = first * head_lane[a] + away
                    key_mix[side, t * tile_heads + a, dst, LANES:] = second

    def mix_values(side):
        for p in range(pairs):
            dst = slice(p * BLOCK, (p + 1) * BLOCK)
            even = slice(2 * p * BLOCK, (2 * p + 1) * BLOCK)
            odd = slice((2 * p + 1) * BLOCK, (2 * p + 2) * BLOCK)
            for t in range(tiles):
                cut = slice(t * LANES, (t + 1) * LANES)
                value_mix[side, t, dst, :LANES] = kv[2 * side + 1, even, cut]
                value_mix[side, t, dst, LANES:] = kv[2 * side + 1, odd, cut]

    def mix_query(query_ref, mask, second):
        second_b = second.astype(BF16)
        first_b = (1.0 - second).astype(BF16)
        mixed = []
        for h in range(HEADS):
            t, a = h // tile_heads, h % tile_heads
            piece = query_ref[:, t * LANES : (t + 1) * LANES] * head_lane[a]
            mixed.append(jnp.concatenate([piece * first_b + mask * other_lane[a], piece * second_b], axis=1))
        return mixed

    def attend(mixed, second, sides):
        parts = []
        for t in range(tiles):
            picked = None
            for a in range(tile_heads):
                h = t * tile_heads + a
                acc = None
                for side in sides:
                    half = dot(mixed[h], key_mix[side, h], (1, 1))
                    weight = (half + half * jnp.tanh(half)).astype(BF16)
                    term = dot(weight, value_mix[side, t], (1, 0))
                    acc = term if acc is None else acc + term
                chosen = jnp.where(second > 0.5, acc[:, LANES:], acc[:, :LANES])
                picked = chosen if a == 0 else jnp.where(lane // head_width == a, chosen, picked)
            parts.append(picked)
        return jnp.concatenate(parts, axis=1)

    own_mixed = mix_query(query_v, own_mask, own_second)
    loads[2].wait()
    mix_keys(0)
    loads[3].wait()
    mix_values(0)
    total[...] = attend(own_mixed, own_second, (0,))
    for copy in pair_copies:
        copy.wait_recv()
    mix_keys(1)
    mix_values(1)

    part_copies = []
    for j in range(1, chips):
        mask_copies[j - 1].wait_recv()
        query_copies[j - 1].wait_recv()
        mask, second = expand(mask_in[j - 1])
        mixed = mix_query(query_in.at[j - 1], mask, second)
        part_out[j - 1] = attend(mixed, second, (0, 1)).astype(BF16)
        part_copies.append(
            remote(part_out.at[j - 1], part_in.at[j - 1], part_send.at[j - 1], part_recv.at[j - 1], x_peer(-j))
        )
        part_copies[-1].start()
    total[...] += attend(own_mixed, own_second, (1,))
    for j in range(1, chips):
        part_copies[j - 1].wait_recv()
        total[...] += part_in[j - 1].astype(F32)

    slice_out[...] = total[...].astype(BF16)
    slice_copies = []
    for k in range(1, depth):
        start = pl.multiple_of(((hist + k) % depth) * chunk, chunk)
        slice_copies.append(
            remote(slice_out.at[pl.ds(start, chunk)], slice_in.at[k - 1], slice_send.at[k - 1], slice_recv.at[k - 1], z_peer(k))
        )
        slice_copies[-1].start()
    mine = pl.ds(pl.multiple_of(hist * chunk, chunk), chunk)
    attended = total[mine, :]
    for k in range(1, depth):
        slice_copies[k - 1].wait_recv()
        attended += slice_in[k - 1].astype(F32)

    mean_square = jnp.mean(attended * attended, axis=-1, keepdims=True)
    normed = (attended * lax.rsqrt(mean_square + 1e-06) * gain[...]).astype(BF16)
    loads[4].wait()
    half = dot(normed, up_v[...], (1, 0)) * 0.5
    hidden = (half + half * jnp.tanh(half)).astype(BF16)
    loads[5].wait()
    result = feats_v[mine, :].astype(F32) + dot(hidden, down_v[...], (1, 0))
    out[mine, :] = result.astype(BF16)
    out_copies = []
    for k in range(1, depth):
        out_copies.append(remote(out.at[mine], out.at[mine], out_send.at[k - 1], out_recv.at[k - 1], z_peer(k)))
        out_copies[-1].start()
    for copy in query_copies + mask_copies + pair_copies + part_copies + slice_copies:
        copy.wait_send()
    for copy in out_copies:
        copy.wait()


def shards(chips, depth, feats, table, cat, lists, count, keys, values, w_query, gain, w_up, w_down):
    rows, width = feats.shape
    hidden = w_up.shape[1]
    history = keys.shape[0]
    chunk = rows // depth
    far, deep = max(chips - 1, 1), max(depth - 1, 1)
    vmem = pl.BlockSpec(memory_space=pltpu.VMEM)
    hbm = pl.BlockSpec(memory_space=pltpu.HBM)
    dma = pltpu.SemaphoreType.DMA
    scratch = [
        pltpu.VMEM((rows, width), BF16),
        pltpu.VMEM((width, width), BF16),
        pltpu.VMEM((width, hidden), BF16),
        pltpu.VMEM((hidden, width), BF16),
        pltpu.VMEM((4, history, width), BF16),
        pltpu.VMEM((2, HEADS, history // 2, 2 * LANES), BF16),
        pltpu.VMEM((2, width // LANES, history // 2, 2 * LANES), BF16),
        pltpu.VMEM((rows, width), BF16),
        pltpu.VMEM((far, rows, width), BF16),
        pltpu.VMEM((chips, 16, rows), BF16),
        pltpu.VMEM((far, 16, rows), BF16),
        pltpu.VMEM((rows, width), F32),
        pltpu.VMEM((far, rows, width), BF16),
        pltpu.VMEM((far, rows, width), BF16),
        pltpu.VMEM((rows, width), BF16),
        pltpu.VMEM((deep, chunk, width), BF16),
        dma((6,)), dma((2,)), dma((2,)),
        dma((far,)), dma((far,)), dma((far,)), dma((far,)), dma((far,)), dma((far,)),
        dma((deep,)), dma((deep,)), dma((deep,)), dma((deep,)),
    ]
    return pl.pallas_call(
        functools.partial(kernel, chips, depth),
        out_shape=jax.ShapeDtypeStruct((rows, width), BF16),
        in_specs=[hbm, vmem, vmem, vmem, vmem, hbm, hbm, hbm, vmem, hbm, hbm],
        out_specs=vmem,
        scratch_shapes=scratch,
        compiler_params=pltpu.CompilerParams(
            collective_id=0, has_side_effects=True, vmem_limit_bytes=48 * 1024 * 1024
        ),
    )(
        feats, table, cat.reshape(1, rows), lists.T, count.reshape(1, rows), keys, values,
        w_query, gain.reshape(1, width), w_up, w_down,
    )


def solution(mesh):
    in_specs = (
        P(("groups", "cand"), None),
        P("groups", None),
        P(("groups", "cand")),
        P(("groups", "cand"), None),
        P(("groups", "cand")),
        P(("groups", "cand", "hist"), None),
        P(("groups", "cand", "hist"), None),
        P(),
        P(),
        P(),
        P(),
    )
    out_specs = P(("groups", "cand"), None)
    body = functools.partial(shards, mesh.shape["cand"] // CORES, mesh.shape["hist"])
    return jax.shard_map(body, mesh=mesh, in_specs=in_specs, out_specs=out_specs, check_vma=False)
```

time: 121 us -> 33.3 us (0.28)
  waiting for transfers between devices: 78.5 us -> 0 us
  Pallas kernels: 0 us -> 24.8 us
  matrix products: 14.3 us -> 0 us
  between operations: 13.5 us -> 0.02 us
  other arithmetic: 3.25 us -> 0 us
  local copies, waits for them, and re-layouts: 10.2 us -> 8.07 us
    ppermute x3 -> x0, waiting for transfers between devices: 41 us -> none  [passed_along(): return lax.ppermute(block, axis, route)]
    psum x1 -> x0, waiting for transfers between devices: 37.5 us -> none  [shards(): attended = lax.psum(partial_sum, 'hist')]
    pallas_call x0 -> x1, Pallas kernels: none -> 24.8 us  [shards(): pl.pallas_call(functools.partial(kernel, chips, depth), out_shape=jax.Sha...]
    dot_general x6 -> x0, matrix products: 14.3 us -> none  [the longest x4 11.4 us: partial_attend(): jnp.einsum('hcj,jhd->chd', weights_bf, value_heads, preferred_element_typ...]
    unnamed x19 -> x23, local copies, waits for them, and re-layouts: 2.17 us -> 8.07 us
    while x18 -> x0, local copies, waits for them, and re-layouts: 3.59 us -> none
    slice x3 -> x0, local copies, waits for them, and re-layouts: 2.6 us -> none  [attend(): kv_piece[0]]
    broadcast_in_dim x4 -> x0, local copies, waits for them, and re-layouts: 1.34 us -> none  [partial_attend(): jnp.broadcast_to(member[:, :, None], (row_count, blocks_here, block_rows))]
  transfers between devices with their start and end apart: 4 -> 0, of which waited for: 4 -> 0; matrix products, arithmetic and copies ran while one was open for 2% -> 0% of each run, Pallas kernels for 0% -> 0%
where the time goes in v1:
time: 33.3 us; the launch traced here: 32.9 us
  Pallas kernels  24.8 us (74%)
  local copies, waits for them, and re-layouts  8.07 us (24%)
    pallas_call x1, Pallas kernels, shards(): pl.pallas_call(functools.partial(kernel, chips, depth), out_shape=jax.Sha...  24.8 us
    unnamed x23, local copies, waits for them, and re-layouts  8.07 us

profile of v1, /device:TPU:0, one launch (start us, length us, event | category | flops | bytes accessed | tf_op | source)
XLA Modules:
  0.0 32.9 jit_solution(1147324540261947444)
XLA Ops:
  0.0 0.0 copy-start.10
  0.0 0.0 copy-start.8
  0.0 0.0 copy-start.9
  0.0 0.0 copy-start.7
  0.0 0.7 %copy-done.10 = f32[256]{0:T(256)S(1)} copy-done((f32[256]{0:T(256)S(1)}, f32[256]{0:T(256)}, u32[]{:S(2)}) %copy-start.10) | copy-done | bytes 1048
  0.7 0.0 copy-done.8
  0.7 0.0 copy-done.9
  0.7 0.0 copy-done.7
  0.7 0.0 copy-start
  0.7 1.0 %copy-done = bf16[1024,256]{1,0:T(8,128)(2,1)S(1)} copy-done((bf16[1024,256]{1,0:T(8,128)(2,1)S(1)}, bf16[1024,256]{1,0:T(8,128)(2,1)}, u32[]{:S(2)}) %copy-start) | copy-done | bytes 524312
  1.8 0.0 copy-start.1
  1.8 1.0 %copy-done.1 = bf16[1024,256]{1,0:T(8,128)(2,1)S(1)} copy-done((bf16[1024,256]{1,0:T(8,128)(2,1)S(1)}, bf16[1024,256]{1,0:T(8,128)(2,1)}, u32[]{:S(2)}) %copy-start.1) | copy-done | bytes 524312
  2.8 0.0 copy-start.2
  2.8 1.0 %copy-done.2 = bf16[256,1024]{1,0:T(8,128)(2,1)S(1)} copy-done((bf16[256,1024]{1,0:T(8,128)(2,1)S(1)}, bf16[256,1024]{1,0:T(8,128)(2,1)}, u32[]{:S(2)}) %copy-start.2) | copy-done | bytes 524312
  3.9 0.0 copy-start.3
  3.9 1.0 %copy-done.3 = bf16[1024,256]{1,0:T(8,128)(2,1)S(1)} copy-done((bf16[1024,256]{1,0:T(8,128)(2,1)S(1)}, bf16[1024,256]{1,0:T(8,128)(2,1)}, u32[]{:S(2)}) %copy-start.3) | copy-done | bytes 524312
  4.9 0.0 copy-start.4
  4.9 0.9 %copy-done.4 = bf16[256,256]{1,0:T(8,128)(2,1)S(1)} copy-done((bf16[256,256]{1,0:T(8,128)(2,1)S(1)}, bf16[256,256]{1,0:T(8,128)(2,1)}, u32[]{:S(2)}) %copy-start.4) | copy-done | bytes 131096
  5.8 0.0 copy-start.5
  5.8 0.9 %copy-done.5 = bf16[256,256]{1,0:T(8,128)(2,1)S(1)} copy-done((bf16[256,256]{1,0:T(8,128)(2,1)S(1)}, bf16[256,256]{1,0:T(8,128)(2,1)}, u32[]{:S(2)}) %copy-start.5) | copy-done | bytes 131096
  6.7 0.0 copy-start.6
  6.7 0.7 %copy-done.6 = s32[256,16]{0,1:T(8,128)S(1)} copy-done((s32[256,16]{0,1:T(8,128)S(1)}, s32[256,16]{0,1:T(8,128)}, u32[]{:S(2)}) %copy-start.6) | copy-done | bytes 16408
  7.4 24.8 %shard_map.109 = bf16[256,256]{1,0:T(8,128)(2,1)S(1)} custom-call(bf16[256,256]{1,0:T(8,128)(2,1)S(1)} %copy-done.4, bf16[2,256]{1,0:T(2,128)(2,1)S(1)} %copy-done.7, s32[1,256]{1,0:T(1,128)S(1)} %bitcast.5, s32[16,256]{1,0:T(8,128)S(1)} %bitcast.4, s32[1,256]{1,0:T(1,128)S(1)} %bitcast.6, bf16[1024,256]{1,0:T(8,128)(2,1)S(1)} %copy-done, ...), custom_call_target="tpu_custom_call" | custom-call | tf_op jit(solution)/shard_map/pallas_call | solution.py:266
  32.3 0.7 %copy.13 = bf16[256,256]{1,0:T(8,128)(2,1)} copy(bf16[256,256]{1,0:T(8,128)(2,1)S(1)} %shard_map.109) | data formatting | bytes 262144
Async XLA Ops:
  0.0 0.7 %copy-start.10 = (f32[256]{0:T(256)S(1)}, f32[256]{0:T(256)}, u32[]{:S(2)}) copy-start(f32[256]{0:T(256)} %param.19) | copy-start | bytes 3076
  0.0 0.7 %copy-start.8 = (s32[256]{0:T(256)S(1)}, s32[256]{0:T(256)}, u32[]{:S(2)}) copy-start(s32[256]{0:T(256)} %param.13) | copy-start | bytes 3076
  0.0 0.7 %copy-start.9 = (s32[256]{0:T(256)S(1)}, s32[256]{0:T(256)}, u32[]{:S(2)}) copy-start(s32[256]{0:T(256)} %param.15) | copy-start | bytes 3076
  0.0 0.7 %copy-start.7 = (bf16[2,256]{1,0:T(2,128)(2,1)S(1)}, bf16[2,256]{1,0:T(2,128)(2,1)}, u32[]{:S(2)}) copy-start(bf16[2,256]{1,0:T(2,128)(2,1)} %table.1) | copy-start | bytes 3076
  0.7 1.0 %copy-start = (bf16[1024,256]{1,0:T(8,128)(2,1)S(1)}, bf16[1024,256]{1,0:T(8,128)(2,1)}, u32[]{:S(2)}) copy-start(bf16[1024,256]{1,0:T(8,128)(2,1)} %keys.1) | copy-start | bytes 1572868
  1.8 1.0 %copy-start.1 = (bf16[1024,256]{1,0:T(8,128)(2,1)S(1)}, bf16[1024,256]{1,0:T(8,128)(2,1)}, u32[]{:S(2)}) copy-start(bf16[1024,256]{1,0:T(8,128)(2,1)} %values.1) | copy-start | bytes 1572868
  2.8 1.0 %copy-start.2 = (bf16[256,1024]{1,0:T(8,128)(2,1)S(1)}, bf16[256,1024]{1,0:T(8,128)(2,1)}, u32[]{:S(2)}) copy-start(bf16[256,1024]{1,0:T(8,128)(2,1)} %w_up.1) | copy-start | bytes 1572868
  3.9 1.0 %copy-start.3 = (bf16[1024,256]{1,0:T(8,128)(2,1)S(1)}, bf16[1024,256]{1,0:T(8,128)(2,1)}, u32[]{:S(2)}) copy-start(bf16[1024,256]{1,0:T(8,128)(2,1)} %w_down.1) | copy-start | bytes 1572868
  4.9 0.9 %copy-start.4 = (bf16[256,256]{1,0:T(8,128)(2,1)S(1)}, bf16[256,256]{1,0:T(8,128)(2,1)}, u32[]{:S(2)}) copy-start(bf16[256,256]{1,0:T(8,128)(2,1)} %feats.1) | copy-start | bytes 393220
  5.8 0.9 %copy-start.5 = (bf16[256,256]{1,0:T(8,128)(2,1)S(1)}, bf16[256,256]{1,0:T(8,128)(2,1)}, u32[]{:S(2)}) copy-start(bf16[256,256]{1,0:T(8,128)(2,1)} %w_query.1) | copy-start | bytes 393220
  6.7 0.7 %copy-start.6 = (s32[256,16]{0,1:T(8,128)S(1)}, s32[256,16]{0,1:T(8,128)}, u32[]{:S(2)}) copy-start(s32[256,16]{0,1:T(8,128)} %param.14) | copy-start | bytes 49156

commit v2 on v1

--- a/solution.py
+++ b/solution.py
@@ -270,7 +270,7 @@
         out_specs=vmem,
         scratch_shapes=scratch,
         compiler_params=pltpu.CompilerParams(
-            collective_id=0, has_side_effects=True, vmem_limit_bytes=48 * 1024 * 1024
+            collective_id=0, has_side_effects=True, vmem_limit_bytes=64000 * 1024
         ),
     )(
         feats, table, cat.reshape(1, rows), lists.T, count.reshape(1, rows), keys, values,

time: 33.3 us -> 28 us (0.84)
  local copies, waits for them, and re-layouts: 8.07 us -> 1.57 us
  Pallas kernels: 24.8 us -> 26.2 us
    unnamed x23 -> x1, local copies, waits for them, and re-layouts: 8.07 us -> 1.57 us
    pallas_call x1, Pallas kernels: 24.8 us -> 26.2 us  [shards(): pl.pallas_call(functools.partial(kernel, chips, depth), out_shape=jax.Sha...]
where the time goes in v2:
time: 28 us; the launch traced here: 27.8 us
  Pallas kernels  26.2 us (94%)
  local copies, waits for them, and re-layouts  1.57 us (6%)
    pallas_call x1, Pallas kernels, shards(): pl.pallas_call(functools.partial(kernel, chips, depth), out_shape=jax.Sha...  26.2 us
    unnamed x1, local copies, waits for them, and re-layouts  1.57 us

profile of v2, /device:TPU:0, one launch (start us, length us, event | category | flops | bytes accessed | tf_op | source)
XLA Modules:
  0.0 27.8 jit_solution(3967332432508321080)
XLA Ops:
  0.0 26.2 %shard_map.109 = bf16[256,256]{1,0:T(8,128)(2,1)} custom-call(bf16[256,256]{1,0:T(8,128)(2,1)} %feats.1, bf16[2,256]{1,0:T(2,128)(2,1)} %table.1, s32[1,256]{1,0:T(1,128)} %bitcast.5, s32[16,256]{1,0:T(8,128)} %bitcast.4, s32[1,256]{1,0:T(1,128)} %bitcast.6, bf16[1024,256]{1,0:T(8,128)(2,1)} %keys.1, bf16[1024,256]{1,0:T(8,128)(2,1)} %values.1, ...), custom_call_target="tpu_custom_call" | custom-call | tf_op jit(solution)/shard_map/pallas_call | solution.py:266
  26.2 1.6 %copy.13 = bf16[256,256]{1,0:T(8,128)(2,1)} copy(bf16[256,256]{1,0:T(8,128)(2,1)} %shard_map.109) | data formatting | bytes 262144
